TPU v7x, 256 devices: a whole 4x4x8 slice. The times are simulated.
256 devices in a mesh: dp: 8 (over y, core), tm: 32 (over z, x).
Axes of the slice: x: 4, y: 4, z: 8, core: 2. Of those that a mesh axis runs over, the one named last changes fastest.
Arguments:
- frames: bfloat16 [65536, 1536], P(('dp', 'tm')), may hold values from -28 to 28, as said below
- seg: int32 [8, 8192], P('dp'), may hold values from 0 to 3, never falling along the last dimension, each value on 1 to 4096 neighbouring positions
- look_back: int32 [8, 32], P('dp'), may hold values 0 or 1
- w_dw: float32 [5, 1536], replicated, may hold values from -2.5 to 2.5
- w_qkv: bfloat16 [1536, 4608], P(None, 'dp'), may hold values from -0.15625 to 0.15625
- w_o: bfloat16 [1536, 1536], replicated, may hold values from -1.5 to 1.5
- cotangent: bfloat16 [65536, 1536], P(('dp', 'tm')), may hold values from -1 to 1
Outputs:
- mixed: bfloat16 [65536, 1536], P(('dp', 'tm'))
- weight_grad: float32 [1536, 1536], P('tm', 'dp')
Inputs may be any that keep to these rules, and one draw needn't show every extreme that they name: Float features; a few short runs of frames may be several times larger than the rest. `seg`: recording numbers never fall along a replica's frames; each recording has 1 to 4096 frames, one exactly 4096.
All inputs are finite; a program needn't handle non-finite values. No bound on the sum of `look_back` on one device may be relied on, other than what follows from the above.
Results may differ from a plain program's by a relative error of at most 0.012.
The roundings to bfloat16 on the way count: a program that leaves them out, or rounds other values in their place, can miss the bound.
Values may be sent and summed in bfloat16 or wider, within the bound.
A program may use at most 128 MiB of HBM per device.

v0:
```python
import math
import jax
import jax.numpy as jnp
from jax import lax
from jax.sharding import PartitionSpec as P

KER = 5
STRETCH = 256


def extended(block, sides, width):
    for axis, dim in sides:
        count = lax.axis_size(axis)
        forward = [(i, i + 1) for i in range(count - 1)]
        backward = [(target, source) for source, target in forward]
        low = lax.ppermute(
            lax.slice_in_dim(block, block.shape[dim] - width, None, axis=dim), axis, forward
        )
        high = lax.ppermute(lax.slice_in_dim(block, 0, width, axis=dim), axis, backward)
        block = jnp.concatenate([low, block, high], axis=dim)
    return block


def swapped(block, axis, distance):
    count = lax.axis_size(axis)
    route = []
    for low in range(count):
        high = low | 1 << distance
        if high != low and high < count:
            route += [(low, high), (high, low)]
    return lax.ppermute(block, axis, route)


def stretch_attention(queries, keys, values, seg_row, look_row, stretch):
    frame_count, heads_here, head_dim = queries.shape
    value_dim = values.shape[2]
    blocks = frame_count // stretch
    query_blocks = queries.reshape(blocks, stretch, heads_here, head_dim)
    key_blocks = keys.reshape(blocks, stretch, heads_here, head_dim)
    value_blocks = values.reshape(blocks, stretch, heads_here, value_dim)
    key_pairs = jnp.concatenate(
        [jnp.concatenate([jnp.zeros_like(key_blocks[:1]), key_blocks[:-1]], 0), key_blocks], 1
    )
    value_pairs = jnp.concatenate(
        [jnp.concatenate([jnp.zeros_like(value_blocks[:1]), value_blocks[:-1]], 0), value_blocks], 1
    )
    seg_blocks = seg_row.reshape(blocks, stretch)
    seg_pairs = jnp.concatenate(
        [jnp.concatenate([jnp.full((1, stretch), -1, jnp.int32), seg_blocks[:-1]], 0), seg_blocks],
        1,
    )
    allow_prev = look_row == 1
    per_step = math.gcd(blocks, max(1, 512 // stretch))
    current = jnp.arange(2 * stretch) >= stretch
    scale = 1.0 / math.sqrt(head_dim)

    def block_step(block_index):
        start = block_index * per_step

        def pick_rows(array):
            return lax.dynamic_slice_in_dim(array, start, per_step, 0)

        scores = (
            jnp.einsum(
                "gqhd,gkhd->ghqk",
                pick_rows(query_blocks),
                pick_rows(key_pairs),
                preferred_element_type=jnp.float32,
            )
            * scale
        )
        same_rec = pick_rows(seg_pairs)[:, None, :] == pick_rows(seg_blocks)[:, :, None]
        allowed = same_rec & (current[None, None, :] | pick_rows(allow_prev)[:, None, None])
        scores = jnp.where(allowed[:, None], scores, -1e30)
        row_max = jnp.max(scores, axis=-1, keepdims=True)
        raw_weights = jnp.exp(scores - row_max)
        probs = (raw_weights / jnp.sum(raw_weights, axis=-1, keepdims=True)).astype(jnp.bfloat16)
        outputs = jnp.einsum(
            "ghqk,gkhv->gqhv", probs, pick_rows(value_pairs), preferred_element_type=jnp.float32
        )
        return outputs.astype(jnp.bfloat16).reshape(per_step * stretch, heads_here * value_dim)

    mixed = lax.map(block_step, jnp.arange(blocks // per_step, dtype=jnp.int32))
    return mixed.reshape(frame_count, heads_here * value_dim)


def local(frames, seg, look_back, w_dw, w_qkv, w_o, cotangent):
    rows = frames.shape[0]
    width = frames.shape[1]
    tm_count = lax.axis_size("tm")
    piece = width // tm_count
    half = KER // 2
    padded = extended(frames, (("tm", 0),), half)
    seg_row = seg[0]
    look_row = look_back[0]
    seg_padded = jnp.pad(seg_row, (half, half), constant_values=-1)
    local_seg = lax.dynamic_slice_in_dim(
        seg_padded, lax.axis_index("tm") * rows, rows + 2 * half, 0
    )
    own_seg = local_seg[half : half + rows]
    total = jnp.zeros((rows, width), jnp.float32)
    for offset in range(KER):
        same_rec = (local_seg[offset : offset + rows] == own_seg).astype(jnp.float32)
        total = (
            total
            + w_dw[offset] * padded[offset : offset + rows].astype(jnp.float32) * same_rec[:, None]
        )
    activ = jax.nn.silu(total).astype(jnp.bfloat16)
    qkv = jnp.dot(
        activ, lax.all_gather(w_qkv, "dp", axis=1, tiled=True), preferred_element_type=jnp.float32
    ).astype(jnp.bfloat16)
    arranged = qkv.reshape(rows, 3, tm_count, piece)
    arrived = lax.all_to_all(arranged, "tm", split_axis=2, concat_axis=0, tiled=True)
    frame_count = arrived.shape[0]
    lower = lax.axis_index("tm") % 2 == 0
    own_pair = arrived[:, 0:2, 0, :]
    other_pair = swapped(own_pair, "tm", 0)
    joined = jnp.where(
        lower,
        jnp.concatenate([own_pair, other_pair], -1),
        jnp.concatenate([other_pair, own_pair], -1),
    )
    queries = joined[:, 0][:, None, :]
    keys = joined[:, 1][:, None, :]
    values = arrived[:, 2, 0, :][:, None, :]
    attended = stretch_attention(queries, keys, values, seg_row, look_row, STRETCH)
    returned = lax.all_to_all(
        attended.reshape(frame_count, 1, piece), "tm", split_axis=0, concat_axis=1, tiled=True
    )
    attn = returned.reshape(rows, width)
    mixed = jnp.dot(attn, w_o, preferred_element_type=jnp.float32).astype(jnp.bfloat16)
    grad_term = lax.dot_general(
        attn, cotangent, (((0,), (0,)), ((), ())), preferred_element_type=jnp.float32
    )
    row_share = lax.psum_scatter(grad_term, "tm", scatter_dimension=0, tiled=True)
    weight_grad = lax.psum_scatter(row_share, "dp", scatter_dimension=1, tiled=True)
    return (mixed, weight_grad)


def solution(mesh):
    placed = (
        P(("dp", "tm"), None),
        P("dp", None),
        P("dp", None),
        P(),
        P(None, "dp"),
        P(),
        P(("dp", "tm"), None),
    )
    return jax.shard_map(
        local,
        mesh=mesh,
        in_specs=placed,
        out_specs=(P(("dp", "tm"), None), P("tm", "dp")),
        check_vma=False,
    )
```

profile of v0, /device:TPU:4, one launch (start us, length us, event | category | flops | bytes accessed | tf_op | source)
XLA Modules:
  0.0 700.8 jit_solution(11983358287464709644)
XLA Ops:
  8.4 2.4 collective-permute-start.1
  10.9 3.4 collective-permute-start
  14.6 2.0 collective-permute-done
  16.6 72.7 %all-gather.2.cloned.1.call-done = bf16[1536,4608]{0,1:T(8,128)(2,1)} async-done(((bf16[1536,576]{0,1:T(8,128)(2,1)}), bf16[1536,4608]{0,1:T(8,128)(2,1)}) %all-gather.2.cloned.1.call-update) | async-done | bytes 14155792 | tf_op jit(solution)/shard_map/all_gather | solution.py:110
  89.4 11.5 %convolution_convert_fusion.1 = bf16[256,4608]{1,0:T(8,128)(2,1)} fusion(bf16[1536,4608]{0,1:T(8,128)(2,1)} %all-gather.2.cloned.1.call-done, bf16[256,1536]{1,0:T(8,128)(2,1)S(1)} %copy-done.4, bf16[2,1536]{1,0:T(2,128)(2,1)S(1)} %collective-permute-done, bf16[258,1536]{1,0:T(8,128)(2,1)S(1)} %constant_dynamic-update-slice_fusion.1, ...), kind=kOutput, calls=%fused_computation.23 | convolution fusion | flops 3636461568 | bytes 18925568 | tf_op jit(solution)/shard_map/dot_general | solution.py:109
  100.8 2.8 copy.24
  103.8 66.5 %all_to_all.33 = bf16[256,3,32,48]{0,3,1,2:T(8,128)(2,1)S(1)} all-to-all(bf16[256,3,32,48]{0,3,1,2:T(8,128)(2,1)S(1)} %copy.25), channel_id=1, replica_groups=mesh['dp'=8,'tm'=32] {'tm'}, dimensions={2} | all-to-all | bytes 4718592 | tf_op jit(solution)/shard_map/all_to_all | solution.py:113
  177.0 1.6 fusion.13
  178.6 29.1 %collective-permute-done.2 = bf16[8192,2,48]{0,2,1:T(8,128)(2,1)} collective-permute-done((bf16[8192,2,48]{0,2,1:T(8,128)(2,1)}, bf16[8192,2,48]{0,2,1:T(8,128)(2,1)}, u32[]{:S(2)}, u32[]{:S(2)}) %collective-permute-start.2) | collective-permute-done | bytes 1572896 | tf_op jit(solution)/shard_map/ppermute | solution.py:31
  207.6 3.8 maximum_select_fusion
  213.0 1.6 copy.44
  214.6 3.6 slice.109
  218.2 1.6 copy.43
  220.6 2.9 fusion.11
  223.5 98.1 %while.11 = (s32[]{:T(128)}, bf16[16,512,48]{1,2,0:T(8,128)(2,1)S(1)}, s32[16]{0:T(128)S(1)}, bf16[32,512,1,48]{1,0,3,2:T(8,128)(2,1)}, s32[32,512]{1,0:T(8,128)...) while((s32[]{:T(128)}, ...), condition=%wide.region_3.4_spmd.clone, body=%wide.region_0.3_spmd.clone.sunk | while | flops 77621248 | bytes 3646681 | solution.py:83
  224.7 1.3 constant_dynamic-slice_fusion.12
  230.9 1.3 constant_dynamic-slice_fusion.12
  237.0 1.3 constant_dynamic-slice_fusion.12
  249.3 1.3 constant_dynamic-slice_fusion.12
  322.5 2.0 copy.34
  324.5 6.2 reshape.89
  331.2 45.2 %reduce.20 = bf16[8192,48]{1,0:T(8,128)(2,1)S(1)} reduce(bf16[8192,1,48]{2,1,0:T(2,128)(2,1)} %reshape.89, bf16[]{:T(256)} %broadcast.84), dimensions={1}, to_apply=%reshape.89.reduce_sub_computation | reduce | bytes 1572866 | tf_op jit(solution)/shard_map/reshape;reshape | solution.py:128
  376.4 4.2 reshape.107
  380.6 27.1 %all_to_all.34 = bf16[32,2,6144]{2,1,0:T(2,128)(2,1)S(1)} all-to-all(bf16[32,2,6144]{2,1,0:T(2,128)(2,1)} %reshape.107), channel_id=1, replica_groups=mesh['dp'=8,'tm'=32] {'tm'}, dimensions={0} | all-to-all | bytes 1572864 | tf_op jit(solution)/shard_map/all_to_all | solution.py:127
  407.7 7.9 %reshape.108 = bf16[8192,1,48]{2,1,0:T(2,128)(2,1)} reshape(bf16[32,2,6144]{2,1,0:T(2,128)(2,1)S(1)} %all_to_all.34) | data formatting | bytes 1572864
  415.5 8.1 %copy.32 = bf16[8192,1,48]{0,2,1:T(8,128)(2,1)S(1)} copy(bf16[8192,1,48]{2,1,0:T(2,128)(2,1)} %reshape.108) | data formatting | bytes 1572864 | tf_op jit(solution)/shard_map/all_to_all | solution.py:127
  424.3 5.0 fusion.34
  429.4 227.5 %reduce-scatter.5.cloned.1.call-done = f32[48,1536]{1,0:T(8,128)} async-done(((f32[1536,1536]{1,0:T(8,128)}), f32[48,1536]{1,0:T(8,128)}) %reduce-scatter.5.cloned.1.call-update) | async-done | bytes 294928 | tf_op jit(solution)/shard_map/reduce_scatter | solution.py:135
  656.9 2.1 copy.35
  659.1 4.6 convolution_convert_fusion.2
  663.7 29.0 %reduce-scatter.7.cloned.1.call-done = f32[192,48]{1,0:T(8,128)} async-done(((f32[1536,48]{1,0:T(8,128)}), f32[192,48]{1,0:T(8,128)}) %reduce-scatter.7.cloned.1.call-update) | async-done | bytes 36880
  692.7 1.6 copy.36
  (275 shorter events, 93.7 us)
Async XLA Ops:
  7.2 417.1 %copy-start = (bf16[256,1536]{1,0:T(8,128)(2,1)S(1)}, bf16[256,1536]{1,0:T(8,128)(2,1)}, u32[]{:S(2)}) copy-start(bf16[256,1536]{1,0:T(8,128)(2,1)} %param.15) | copy-start | bytes 2359300
  7.2 1.2 copy-start.4
  7.2 7.1 %copy-start.7 = (s32[1,8192]{1,0:T(1,128)S(1)}, s32[1,8192]{1,0:T(1,128)}, u32[]{:S(2)}) copy-start(s32[1,8192]{1,0:T(1,128)} %param.10) | copy-start | bytes 98308
  7.2 7.3 %copy-start.8 = (f32[5,1536]{1,0:T(8,128)S(1)}, f32[5,1536]{1,0:T(8,128)}, u32[]{:S(2)}) copy-start(f32[5,1536]{1,0:T(8,128)} %param.12) | copy-start | bytes 92164
  7.2 82.2 %all-gather.2.cloned.1.call-start = ((), (), s32[]{:S(2)}) async-start(), calls=%async_computation.4 | async-start | bytes 15925248 | tf_op jit(solution)/shard_map/all_gather | solution.py:110
  7.9 649.0 %reduce-scatter.5.cloned.1.call-start = ((), (), s32[]{:S(2)}) async-start(), calls=%async_computation.5 | async-start | bytes 9732096 | tf_op jit(solution)/shard_map/reduce_scatter | solution.py:135
  8.4 6.2 collective-permute-start.1
  10.9 5.8 collective-permute-start
  170.6 3.8 copy-start.9
  171.9 35.8 %collective-permute-start.2 = (bf16[8192,2,48]{0,2,1:T(8,128)(2,1)}, bf16[8192,2,48]{0,2,1:T(8,128)(2,1)}, u32[]{:S(2)}, u32[]{:S(2)}) collective-permute-start(bf16[8192,2,48]{0,2,1:T(8,128)(2,1)} %slice_bitcast_fusion), channel_id=1, source_target_pairs={{0,1},{1,0},{2,3},{3,2},{4,5},{5,4},{6,7},{7,6},{8,9},{9,8},{10,11... | collective-permute-start | bytes 4718600 | tf_op jit(solution)/shard_map/ppermute | solution.py:31
  175.4 1.1 copy-start.3
  218.2 1.6 copy-start.1
  218.2 2.4 copy-start.2
  220.6 2.9 copy-start.5
  321.6 0.9 copy-start.6
  429.3 263.3 %reduce-scatter.7.cloned.1.call-start = ((), (), s32[]{:S(2)}) async-start(), calls=%async_computation.6 | async-start | bytes 884736
Sparse Core Ops, SparseCore 0:
  9.9 79.4 all-gather.1
  429.5 227.4 reduce-scatter.4
  659.5 33.1 reduce-scatter.6
where the time goes:
time: 704 us; the launch traced here: 701 us
  waiting for transfers between devices  361 us (51%)
  local copies, waits for them, and re-layouts  121 us (17%)
  blocking collectives  93.6 us (13%)
  other arithmetic  55.5 us (8%)
  matrix products  36.9 us (5%)
  between operations  14 us (2%)
  loops' own time  11.7 us (2%)
  starting transfers between devices  7.23 us (1%)
    reduce_scatter x1, waiting for transfers between devices, local(): lax.psum_scatter(grad_term, 'tm', scatter_dimension=0, tiled=True)  228 us
    all_gather x1, waiting for transfers between devices, local(): lax.all_gather(w_qkv, 'dp', axis=1, tiled=True)  72.7 us
    all_to_all x1, blocking collectives, local(): lax.all_to_all(arranged, 'tm', split_axis=2, concat_axis=0, tiled=True)  66.5 us
    dynamic_slice x96, local copies, waits for them, and re-layouts, pick_rows(): return lax.dynamic_slice_in_dim(array, start, per_step, 0)  58.5 us
    another operation x1, other arithmetic, local(): attended.reshape(frame_count, 1, piece)  45.2 us
    unnamed x4, waiting for transfers between devices  29.7 us
    ppermute x1, waiting for transfers between devices, swapped(): return lax.ppermute(block, axis, route)  29.1 us
    all_to_all x1, blocking collectives, local(): lax.all_to_all(attended.reshape(frame_count, 1, piece), 'tm', split_axis=...  27.1 us
  transfers between devices with their start and end apart: 6, of which 5 were waited for; matrix products, arithmetic and copies ran while one was open for 1% of the time, Pallas kernels for 0%

commit v1 on v0

--- a/solution.py
+++ b/solution.py
@@ -107,7 +107,11 @@
         )
     activ = jax.nn.silu(total).astype(jnp.bfloat16)
     qkv = jnp.dot(
-        activ, lax.all_gather(w_qkv, "dp", axis=1, tiled=True), preferred_element_type=jnp.float32
+        activ,
+        jnp.concatenate(
+            lax.all_to_all(jnp.stack([w_qkv] * lax.axis_size("dp")), "dp", 0, 0), axis=1
+        ),
+        preferred_element_type=jnp.float32,
     ).astype(jnp.bfloat16)
     arranged = qkv.reshape(rows, 3, tm_count, piece)
     arrived = lax.all_to_all(arranged, "tm", split_axis=2, concat_axis=0, tiled=True)

time: 704 us -> 789 us (1.12)
  waiting for transfers between devices: 361 us -> 432 us
    all_to_all x0 -> x1, waiting for transfers between devices: none -> 148 us  [local(): lax.all_to_all(jnp.stack([w_qkv] * lax.axis_size('dp')), 'dp', 0, 0)]
    all_gather x1 -> x0, waiting for transfers between devices: 72.7 us -> none  [local(): lax.all_gather(w_qkv, 'dp', axis=1, tiled=True)]
    unnamed x30 -> x28, local copies, waits for them, and re-layouts: 22.9 us -> 20.6 us
    unnamed x4 -> x3, waiting for transfers between devices: 29.7 us -> 29.2 us
where the time goes in v1:
time: 789 us; the launch traced here: 786 us
  waiting for transfers between devices  432 us (55%)
  local copies, waits for them, and re-layouts  128 us (16%)
  blocking collectives  94.7 us (12%)
  other arithmetic  55.5 us (7%)
  matrix products  36.8 us (5%)
  between operations  14.4 us (2%)
  starting transfers between devices  12.8 us (2%)
  loops' own time  11.9 us (2%)
    reduce_scatter x1, waiting for transfers between devices, local(): lax.psum_scatter(grad_term, 'tm', scatter_dimension=0, tiled=True)  227 us
    all_to_all x1, waiting for transfers between devices, local(): lax.all_to_all(jnp.stack([w_qkv] * lax.axis_size('dp')), 'dp', 0, 0)  148 us
    all_to_all x1, blocking collectives, local(): lax.all_to_all(arranged, 'tm', split_axis=2, concat_axis=0, tiled=True)  67.4 us
    dynamic_slice x96, local copies, waits for them, and re-layouts, pick_rows(): return lax.dynamic_slice_in_dim(array, start, per_step, 0)  58.5 us
    another operation x1, other arithmetic, local(): attended.reshape(frame_count, 1, piece)  45.2 us
    unnamed x3, waiting for transfers between devices  29.2 us
    all_to_all x1, blocking collectives, local(): lax.all_to_all(attended.reshape(frame_count, 1, piece), 'tm', split_axis=...  27.4 us
    ppermute x1, waiting for transfers between devices, swapped(): return lax.ppermute(block, axis, route)  26.6 us
  transfers between devices with their start and end apart: 6, of which 5 were waited for; matrix products, arithmetic and copies ran while one was open for 1% of the time, Pallas kernels for 0%

profile of v1, /device:TPU:4, one launch (start us, length us, event | category | flops | bytes accessed | tf_op | source)
XLA Modules:
  0.0 786.1 jit_solution(8862140214266733995)
XLA Ops:
  7.2 7.2 stack.2
  14.4 5.6 all-to-all-start
  20.1 3.1 collective-permute-start
  23.2 2.7 collective-permute-start.1
  26.3 2.4 collective-permute-done.1
  28.7 147.7 %all-to-all-done = bf16[8,1536,576]{1,2,0:T(8,128)(2,1)} async-done(((bf16[8,1536,576]{1,2,0:T(8,128)(2,1)}), bf16[8,1536,576]{1,2,0:T(8,128)(2,1)}, u32[]{:S(2)}, u32[]{:S(2)}) %all-to-all-start) | async-done | bytes 14155808 | tf_op jit(solution)/shard_map/all_to_all | solution.py:112
  176.4 11.5 %convolution_convert_fusion.1 = bf16[256,4608]{1,0:T(8,128)(2,1)} fusion(bf16[1536,4608]{0,1:T(8,128)(2,1)} %bitcast.2, bf16[256,1536]{1,0:T(8,128)(2,1)S(1)} %copy-done.3, bf16[2,1536]{1,0:T(2,128)(2,1)S(1)} %collective-permute-done, bf16[258,1536]{1,0:T(8,128)(2,1)S(1)} %constant_dynamic-update-slice_fusion.1, f32[256]{0:T(256)S(1)} %get-tuple-element.134, ...), kind=kOutput, calls=%fused_computation.23 | convolution fusion | flops 3636461568 | bytes 18925568 | tf_op jit(solution)/shard_map/dot_general | solution.py:109
  187.8 2.8 copy.25
  190.8 67.4 %all_to_all.38 = bf16[256,3,32,48]{0,3,1,2:T(8,128)(2,1)S(1)} all-to-all(bf16[256,3,32,48]{0,3,1,2:T(8,128)(2,1)S(1)} %copy.26), channel_id=1, replica_groups=mesh['dp'=8,'tm'=32] {'tm'}, dimensions={2} | all-to-all | bytes 4718592 | tf_op jit(solution)/shard_map/all_to_all | solution.py:117
  264.1 1.7 slice.102
  266.0 1.6 fusion.13
  267.6 26.6 %collective-permute-done.2 = bf16[8192,2,48]{0,2,1:T(8,128)(2,1)} collective-permute-done((bf16[8192,2,48]{0,2,1:T(8,128)(2,1)}, bf16[8192,2,48]{0,2,1:T(8,128)(2,1)}, u32[]{:S(2)}, u32[]{:S(2)}) %collective-permute-start.2) | collective-permute-done | bytes 1572896 | tf_op jit(solution)/shard_map/ppermute | solution.py:31
  294.1 3.8 maximum_select_fusion
  299.5 1.6 copy.44
  301.1 3.6 slice.109
  306.1 2.9 fusion.11
  309.0 98.2 %while.11 = (s32[]{:T(128)}, bf16[16,512,48]{1,2,0:T(8,128)(2,1)S(1)}, s32[16]{0:T(128)S(1)}, bf16[32,512,1,48]{1,0,3,2:T(8,128)(2,1)}, s32[32,512]{1,0:T(8,128)...) while((s32[]{:T(128)}, ...), condition=%wide.region_3.4_spmd.clone, body=%wide.region_0.3_spmd.clone.sunk | while | flops 77621248 | bytes 3646689 | solution.py:83
  310.4 1.3 constant_dynamic-slice_fusion.12
  316.5 1.3 constant_dynamic-slice_fusion.12
  408.1 2.0 copy.35
  410.0 6.2 reshape.99
  416.7 45.2 %reduce.20 = bf16[8192,48]{1,0:T(8,128)(2,1)S(1)} reduce(bf16[8192,1,48]{2,1,0:T(2,128)(2,1)} %reshape.99, bf16[]{:T(256)} %broadcast.86), dimensions={1}, to_apply=%reshape.99.reduce_sub_computation | reduce | bytes 1572866 | tf_op jit(solution)/shard_map/reshape;reshape | solution.py:132
  462.0 4.2 reshape.117
  466.2 27.4 %all_to_all.39 = bf16[32,2,6144]{2,1,0:T(2,128)(2,1)S(1)} all-to-all(bf16[32,2,6144]{2,1,0:T(2,128)(2,1)} %reshape.117), channel_id=1, replica_groups=mesh['dp'=8,'tm'=32] {'tm'}, dimensions={0} | all-to-all | bytes 1572864 | tf_op jit(solution)/shard_map/all_to_all | solution.py:131
  493.6 7.9 %reshape.118 = bf16[8192,1,48]{2,1,0:T(2,128)(2,1)} reshape(bf16[32,2,6144]{2,1,0:T(2,128)(2,1)S(1)} %all_to_all.39) | data formatting | bytes 1572864
  501.4 8.1 %copy.33 = bf16[8192,1,48]{0,2,1:T(8,128)(2,1)S(1)} copy(bf16[8192,1,48]{2,1,0:T(2,128)(2,1)} %reshape.118) | data formatting | bytes 1572864 | tf_op jit(solution)/shard_map/all_to_all | solution.py:131
  510.2 5.0 fusion.34
  515.3 226.5 %reduce-scatter.5.cloned.1.call-done = f32[48,1536]{1,0:T(8,128)} async-done(((f32[1536,1536]{1,0:T(8,128)}), f32[48,1536]{1,0:T(8,128)}) %reduce-scatter.5.cloned.1.call-update) | async-done | bytes 294928 | tf_op jit(solution)/shard_map/reduce_scatter | solution.py:139
  741.8 2.1 copy.36
  743.9 4.6 convolution_convert_fusion.2
  748.6 29.1 %reduce-scatter.7.cloned.1.call-done = f32[192,48]{1,0:T(8,128)} async-done(((f32[1536,48]{1,0:T(8,128)}), f32[192,48]{1,0:T(8,128)}) %reduce-scatter.7.cloned.1.call-update) | async-done | bytes 36880
  777.7 1.6 copy.37
  (273 shorter events, 95.1 us)
Async XLA Ops:
  7.2 503.0 %copy-start = (bf16[256,1536]{1,0:T(8,128)(2,1)S(1)}, bf16[256,1536]{1,0:T(8,128)(2,1)}, u32[]{:S(2)}) copy-start(bf16[256,1536]{1,0:T(8,128)(2,1)} %param.15) | copy-start | bytes 2359300
  14.3 5.7 copy-start.3
  14.3 11.6 %copy-start.6 = (s32[1,8192]{1,0:T(1,128)S(1)}, s32[1,8192]{1,0:T(1,128)}, u32[]{:S(2)}) copy-start(s32[1,8192]{1,0:T(1,128)} %param.10) | copy-start | bytes 98308
  14.4 162.0 %all-to-all-start = ((bf16[8,1536,576]{1,2,0:T(8,128)(2,1)}), bf16[8,1536,576]{1,2,0:T(8,128)(2,1)}, u32[]{:S(2)}, u32[]{:S(2)}) async-start(bf16[8,1536,576]{1,2,0:T(8,128)(2,1)} %stack.2), calls=%async_computation | async-start | bytes 28311552 | tf_op jit(solution)/shard_map/all_to_all | solution.py:112
  20.0 6.2 copy-start.7
  20.0 721.8 %reduce-scatter.5.cloned.1.call-start = ((), (), s32[]{:S(2)}) async-start(), calls=%async_computation.5 | async-start | bytes 9732096 | tf_op jit(solution)/shard_map/reduce_scatter | solution.py:139
  20.1 8.7 %collective-permute-start = (bf16[2,1536]{1,0:T(2,128)(2,1)S(1)}, bf16[2,1536]{1,0:T(2,128)(2,1)S(1)}, u32[]{:S(2)}, u32[]{:S(2)}) collective-permute-start(bf16[2,1536]{1,0:T(2,128)(2,1)S(1)} %get-tuple-element.130), channel_id=1, source_target_pairs={{0,1},{1,2},{2,3},{3,4},{4,5},{5,6},{6,7},{7,8},{8,9},{9,10},{10,1... | collective-permute-start | bytes 18440 | tf_op jit(solution)/shard_map/ppermute | solution.py:16
  23.2 5.5 collective-permute-start.1
  258.4 3.7 copy-start.8
  259.7 34.4 %collective-permute-start.2 = (bf16[8192,2,48]{0,2,1:T(8,128)(2,1)}, bf16[8192,2,48]{0,2,1:T(8,128)(2,1)}, u32[]{:S(2)}, u32[]{:S(2)}) collective-permute-start(bf16[8192,2,48]{0,2,1:T(8,128)(2,1)} %slice_bitcast_fusion), channel_id=1, source_target_pairs={{0,1},{1,0},{2,3},{3,2},{4,5},{5,4},{6,7},{7,6},{8,9},{9,8},{10,11... | collective-permute-start | bytes 4718600 | tf_op jit(solution)/shard_map/ppermute | solution.py:31
  264.1 1.7 copy-start.2
  304.7 1.4 copy-start.1
  306.1 2.9 copy-start.4
  407.2 0.9 copy-start.5
  515.2 262.5 %reduce-scatter.7.cloned.1.call-start = ((), (), s32[]{:S(2)}) async-start(), calls=%async_computation.6 | async-start | bytes 884736
Sparse Core Ops, SparseCore 0:
  515.3 226.4 reduce-scatter.4
  744.3 33.3 reduce-scatter.6
